TPU v7x, 128 devices: a whole 4x4x4 slice. The times are simulated.
128 devices in a mesh: field: 4 (over y_hi, core), space: 32 (over y_lo, x, z).
Axes of the slice: x: 4, y: 4 (y_hi: 2, y_lo: 2; y = y_hi * 2 + y_lo), z: 4, core: 2. Of those that a mesh axis runs over, the one named last changes fastest.
Arguments:
- fields: float32 [8, 22, 128, 32, 256], P('field', None, 'space'), may hold values from -6 to 6
- velocity: float32 [3, 128, 32, 256], P(None, 'space'), may hold values from -1 to 1
- noise: int32 [2, 2, 8, 3, 128, 32, 256], P(None, None, 'field', None, 'space'), may hold values from -1 to 1
- mixing_rate: float32 [128, 32, 256], P('space'), may hold values from 0.5 to 2
- parcel_cell: int32 [4, 32768], P('field', 'space'), may hold values from 0 to 32767
- parcel_mass: float32 [4, 32768], P('field', 'space'), may hold values from 0.5 to 2
- parcel_temp: float32 [4, 32768], P('field', 'space'), may hold values from 0.5 to 1.5
Outputs:
- new_fields: float32 [8, 22, 128, 32, 256], P('field', None, 'space')
- new_mass: float32 [4, 32768], P('field', 'space')
- new_temp: float32 [4, 32768], P('field', 'space')
Inputs may be any that keep to these rules, and one draw needn't show every extreme that they name: parcel_cell is the parcel's cell within its block of 4 x 32 x 256 cells, ((x - first plane of the block) * 32 + y) * 256 + z; parcels of group g and block b stand in row g, columns b * 1024 to (b + 1) * 1024 - 1. `noise`: wiener increments in units of the substep's scale.
All inputs are finite; a program needn't handle non-finite values.
Results may differ from a plain program's by a relative error of at most 0.0001.
Values sent between devices are 32-bit elements; how exact they have to be, the bound alone decides.
A program may use at most 192 MiB of HBM per device.

v0:
```python
import jax
import jax.numpy as jnp
from jax import lax
from jax.sharding import PartitionSpec as P

STEPS = 2


sub_time = 0.2
diffusivity = 0.1
noise_gain = 0.2
step_time = 0.4
latent_heat = 0.5


def with_halo(array, sides, width):
    for axis, dim in sides:
        peers, length = (lax.axis_size(axis), array.shape[dim])
        up = [(i, (i + 1) % peers) for i in range(peers)]
        down = [(j, i) for i, j in up]
        last = lax.slice_in_dim(array, length - width, length, axis=dim)
        first = lax.slice_in_dim(array, 0, width, axis=dim)
        before = lax.ppermute(last, axis, up)
        after = lax.ppermute(first, axis, down)
        array = jnp.concatenate([before, array, after], axis=dim)
    return array


def advance(padded, velocity, noise_now):
    center = padded[:, :, 1:-1]
    neighbours = [
        (padded[:, :, :-2], padded[:, :, 2:]),
        (jnp.roll(center, 1, 3), jnp.roll(center, -1, 3)),
        (jnp.roll(center, 1, 4), jnp.roll(center, -1, 4)),
    ]
    advect = jnp.zeros_like(center)
    spread = -6.0 * center
    stirred = jnp.zeros_like(center)
    for direction in range(3):
        lower_side, upper_side = neighbours[direction]
        speed_now = velocity[direction][None, None]
        advect = (
            advect
            + jnp.maximum(speed_now, 0.0) * (center - lower_side)
            + jnp.minimum(speed_now, 0.0) * (upper_side - center)
        )
        spread = spread + lower_side + upper_side
        stirred = stirred + 0.5 * (upper_side - lower_side) * noise_now[:, direction][
            :, None
        ].astype(jnp.float32)
    return center + sub_time * (diffusivity * spread - advect) + noise_gain * stirred


def evaporate(mass, temper, vapor, gas_heat):
    sat_frac = 0.8 * jax.nn.sigmoid(4.0 * (temper - 1.0))
    drive = jnp.maximum(sat_frac - vapor, 0.0) / (1.0 - sat_frac)
    rate_now = mass * jnp.log1p(drive)
    heat_now = rate_now * (gas_heat - latent_heat)
    return (
        rate_now,
        heat_now,
        mass - step_time * rate_now,
        temper + step_time * (gas_heat - temper),
    )


def relax(moved, mean_field, mixing_rate, sources):
    mixed = moved - step_time * mixing_rate * (moved - mean_field)
    return mixed.at[:, 0:2].add(step_time * sources[None])


def deposit(cells, rate_now, heat_now, count_cells, plane_shape):
    flat_cells = cells.reshape(-1)
    stacked = jnp.stack(
        [
            jax.ops.segment_sum(rate_now.reshape(-1), flat_cells, num_segments=count_cells),
            jax.ops.segment_sum(heat_now.reshape(-1), flat_cells, num_segments=count_cells),
        ]
    )
    return stacked.reshape((2,) + plane_shape)


def on_device(fields, velocity, noise, mixing_rate, parcel_cell, parcel_mass, parcel_temp):
    plane_shape = fields.shape[2:]
    count_cells = plane_shape[0] * plane_shape[1] * plane_shape[2]
    count_fields = fields.shape[0] * lax.axis_size("field")
    mass_now, temp_now = (parcel_mass, parcel_temp)
    for step in range(STEPS):
        for sub_step in range(2):
            padded = with_halo(fields, (("space", 2),), 1)
            fields = advance(padded, velocity, noise[step, sub_step])
        total = lax.psum(jnp.sum(fields, axis=0), "field")
        mean_field = total / count_fields
        vapor = mean_field[0].reshape(-1)[parcel_cell]
        gas_heat = mean_field[1].reshape(-1)[parcel_cell]
        rate_now, heat_now, mass_now, temp_now = evaporate(mass_now, temp_now, vapor, gas_heat)
        local_sources = deposit(parcel_cell, rate_now, heat_now, count_cells, plane_shape)
        sources = lax.psum(local_sources, "field")
        fields = relax(fields, mean_field, mixing_rate, sources)
    return (fields, mass_now, temp_now)


def solution(mesh):
    placed = (
        P("field", None, "space", None, None),
        P(None, "space", None, None),
        P(None, None, "field", None, "space", None, None),
        P("space", None, None),
        P("field", "space"),
        P("field", "space"),
        P("field", "space"),
    )
    return jax.shard_map(
        on_device,
        mesh=mesh,
        in_specs=placed,
        out_specs=(P("field", None, "space", None, None), P("field", "space"), P("field", "space")),
        check_vma=False,
    )
```

profile of v0, /device:TPU:1, one launch (start us, length us, event | category | flops | bytes accessed | tf_op | source)
XLA Modules:
  0.0 550.3 jit_solution(8918852209742364354)
XLA Ops:
  25.9 5.8 %fusion.81 = (f32[2,22,4,31,256]{4,3,2,1,0:T(8,128)}, f32[2,22,4,31,256]{4,3,2,1,0:T(8,128)}) fusion(f32[2,22,4,32,256]{4,3,2,1,0:T(8,128)S(1)} %copy-done.3), kind=kLoop, calls=%fused_computation.162 | loop fusion | bytes 22347776 | tf_op jit(solution)/shard_map/jit(_roll_static)/slice | solution.py:33
  31.7 6.4 %fusion.83 = (f32[2,22,4,32,255]{4,3,2,1,0:T(8,128)}, f32[2,22,4,32,255]{4,3,2,1,0:T(8,128)}) fusion(f32[2,22,4,32,256]{4,3,2,1,0:T(8,128)S(1)} %copy-done.3), kind=kLoop, calls=%fused_computation.164 | loop fusion | bytes 22978560 | tf_op jit(solution)/shard_map/jit(_roll_static)/slice | solution.py:34
  38.0 12.5 %collective-permute-done = f32[2,22,1,32,256]{4,3,2,1,0:T(8,128)} collective-permute-done((f32[2,22,1,32,256]{4,3,2,1,0:T(8,128)}, f32[2,22,1,32,256]{4,3,2,1,0:T(8,128)}, u32[]{:S(2)}, u32[]{:S(2)}) %collective-permute-start) | collective-permute-done | bytes 1441824 | tf_op jit(solution)/shard_map/ppermute | solution.py:23
  50.6 16.9 %multiply_add_fusion.3 = f32[2,22,4,32,256]{4,3,2,1,0:T(8,128)S(1)} fusion(f32[2,22,4,32,256]{4,3,2,1,0:T(8,128)} %param.11, f32[2,22,1,32,256]{4,3,2,1,0:T(8,128)} %collective-permute-done.1, f32[2,22,4,32,1]{4,3,2,1,0:T(8,128)} %get-tuple-element.72, f32[2,22,4,32,255]{4,3,2,1,0:T(8,128)} %get-tuple-element.74, ...), kind=kLoop, calls=%fused_computation.58 | loop fusion | flops 63438848 | bytes 39059456 | tf_op jit(solution)/shard_map/add | solution.py:51
  72.0 5.8 %collective-permute-start.3 = (f32[2,22,1,32,256]{4,3,2,1,0:T(8,128)}, f32[2,22,1,32,256]{4,3,2,1,0:T(8,128)}, u32[]{:S(2)}, u32[]{:S(2)}) collective-permute-start(f32[2,22,1,32,256]{4,3,2,1,0:T(8,128)} %get-tuple-element.56), channel_id=1, source_target_pairs={{1,0},{2,1},{3,2},{4,3},{5,4},{6,5},{7,6},{8,7},{9,8},{10,9},{11,1... | collective-permute-start | bytes 4325384 | tf_op jit(solution)/shard_map/ppermute | solution.py:24
  78.7 5.7 %fusion.76 = (f32[2,22,4,31,256]{4,3,2,1,0:T(8,128)}, f32[2,22,4,31,256]{4,3,2,1,0:T(8,128)}) fusion(f32[2,22,4,32,256]{4,3,2,1,0:T(8,128)S(1)} %multiply_add_fusion.3), kind=kLoop, calls=%fused_computation.157 | loop fusion | bytes 22347776 | tf_op jit(solution)/shard_map/jit(_roll_static)/slice | solution.py:33
  84.4 6.4 %fusion.78 = (f32[2,22,4,32,255]{4,3,2,1,0:T(8,128)}, f32[2,22,4,32,255]{4,3,2,1,0:T(8,128)}) fusion(f32[2,22,4,32,256]{4,3,2,1,0:T(8,128)S(1)} %multiply_add_fusion.3), kind=kLoop, calls=%fused_computation.159 | loop fusion | bytes 22978560 | tf_op jit(solution)/shard_map/jit(_roll_static)/slice | solution.py:34
  90.8 17.5 %collective-permute-done.2 = f32[2,22,1,32,256]{4,3,2,1,0:T(8,128)} collective-permute-done((f32[2,22,1,32,256]{4,3,2,1,0:T(8,128)}, f32[2,22,1,32,256]{4,3,2,1,0:T(8,128)}, u32[]{:S(2)}, u32[]{:S(2)}) %collective-permute-start.2) | collective-permute-done | bytes 1441824 | tf_op jit(solution)/shard_map/ppermute | solution.py:23
  108.4 17.5 %fusion.63 = (f32[22,4,32,256]{3,2,1,0:T(8,128)}, f32[2,22,4,32,256]{4,3,2,1,0:T(8,128)}) fusion(f32[2,4,32,256]{3,2,1,0:T(8,128)} %get-tuple-element.90, f32[2,4,32,256]{3,2,1,0:T(8,128)} %get-tuple-element.91, f32[2,4,32,256]{3,2,1,0:T(8,128)S(1)} %get-tuple-element.89, f32[2,22,4,32,256]{4,3,2,1,0:T(8,128)S(1)} %multiply_add_fusion.3, ...), kind=kLoop, calls=%fused_computation.144 | loop fusion | flops 64159744 | bytes 41943040 | tf_op jit(solution)/shard_map/reduce_sum | solution.py:92
  131.6 68.9 %all-reduce.5.cloned.1.call-done = f32[22,4,32,256]{3,2,1,0:T(8,128)} async-done(((f32[22,4,32,256]{3,2,1,0:T(8,128)}), f32[22,4,32,256]{3,2,1,0:T(8,128)}) %all-reduce.5.cloned.1.call-update) | async-done | bytes 2883600 | tf_op jit(solution)/shard_map/psum | solution.py:92
  202.8 10.5 %gather_fusion = f32[1024]{0:T(1024)} fusion(f32[32768]{0:T(1024)S(1)} %bitcast.62, s32[1024]{0:T(1024)S(1)} %broadcast_clamp_fusion), kind=kCustom, calls=%fused_computation | custom fusion | bytes 12288 | tf_op jit(solution)/shard_map/gather | solution.py:94
  213.3 6.1 %gather_fusion.1 = f32[1024]{0:T(1024)S(1)} fusion(f32[32768]{0:T(1024)S(1)} %bitcast.63, s32[1024]{0:T(1024)S(1)} %broadcast_clamp_fusion), kind=kCustom, calls=%fused_computation.1 | custom fusion | bytes 12288 | tf_op jit(solution)/shard_map/gather | solution.py:95
  220.9 6.1 %scatter_custom_fusion = f32[32768]{0:T(1024)S(1)} fusion(s32[1024]{0:T(1024)} %bitcast.80, f32[1024]{0:T(1024)} %bitcast.75, f32[]{:T(128)} %constant.72.clone.1), kind=kCustom, calls=%fused_computation.128 | custom fusion | flops 1024 | bytes 131584 | tf_op jit(solution)/shard_map/scatter-add | solution.py:76
  227.7 6.1 %scatter_custom_fusion.1 = f32[32768]{0:T(1024)S(1)} fusion(s32[1024]{0:T(1024)} %bitcast.81, f32[1024]{0:T(1024)} %bitcast.84, f32[]{:T(128)} %constant.72.clone.1), kind=kCustom, calls=%fused_computation.126 | custom fusion | flops 1024 | bytes 131584 | tf_op jit(solution)/shard_map/scatter-add | solution.py:77
  236.5 6.5 %multiply_subtract_fusion.1 = f32[2,22,4,32,256]{4,3,2,1,0:T(8,128)} fusion(f32[2,22,4,32,256]{4,3,2,1,0:T(8,128)} %get-tuple-element.34, f32[22,4,32,256]{3,2,1,0:T(8,128)S(1)} %broadcast_multiply_fusion.1, f32[4,32,256]{2,1,0:T(8,128)S(1)} %copy-done.11), kind=kLoop, calls=%fused_computation.49 | loop fusion | flops 4325376 | bytes 14548992 | tf_op jit(solution)/shard_map/sub | solution.py:68
  243.0 33.4 %all-reduce.7.cloned.1.call-done = f32[2,4,32,256]{3,2,1,0:T(8,128)} async-done(((f32[2,4,32,256]{3,2,1,0:T(8,128)}), f32[2,4,32,256]{3,2,1,0:T(8,128)}) %all-reduce.7.cloned.1.call-update) | async-done | bytes 262160 | tf_op jit(solution)/shard_map/psum | solution.py:98
  293.3 5.8 %fusion.71 = (f32[2,22,4,31,256]{4,3,2,1,0:T(8,128)}, f32[2,22,4,31,256]{4,3,2,1,0:T(8,128)}) fusion(f32[2,22,4,32,256]{4,3,2,1,0:T(8,128)S(1)} %copy-done), kind=kLoop, calls=%fused_computation.152 | loop fusion | bytes 22347776 | tf_op jit(solution)/shard_map/jit(_roll_static)/slice | solution.py:33
  299.0 6.4 %fusion.73 = (f32[2,22,4,32,255]{4,3,2,1,0:T(8,128)}, f32[2,22,4,32,255]{4,3,2,1,0:T(8,128)}) fusion(f32[2,22,4,32,256]{4,3,2,1,0:T(8,128)S(1)} %copy-done), kind=kLoop, calls=%fused_computation.154 | loop fusion | bytes 22978560 | tf_op jit(solution)/shard_map/jit(_roll_static)/slice | solution.py:34
  305.4 18.8 %collective-permute-done.4 = f32[2,22,1,32,256]{4,3,2,1,0:T(8,128)} collective-permute-done((f32[2,22,1,32,256]{4,3,2,1,0:T(8,128)}, f32[2,22,1,32,256]{4,3,2,1,0:T(8,128)}, u32[]{:S(2)}, u32[]{:S(2)}) %collective-permute-start.4) | collective-permute-done | bytes 1441824 | tf_op jit(solution)/shard_map/ppermute | solution.py:23
  324.2 15.2 %multiply_add_fusion.1 = f32[2,22,4,32,256]{4,3,2,1,0:T(8,128)S(1)} fusion(f32[2,22,4,32,256]{4,3,2,1,0:T(8,128)S(1)} %copy-done, f32[2,22,1,32,256]{4,3,2,1,0:T(8,128)} %collective-permute-done.5, f32[2,22,4,32,1]{4,3,2,1,0:T(8,128)} %get-tuple-element.52, f32[2,22,4,32,255]{4,3,2,1,0:T(8,128)} %get-tuple-element.54, ...), kind=kLoop, calls=%fused_computation.41 | loop fusion | flops 63438848 | bytes 39059456 | tf_op jit(solution)/shard_map/add | solution.py:51
  344.4 5.9 %collective-permute-start.7 = (f32[2,22,1,32,256]{4,3,2,1,0:T(8,128)}, f32[2,22,1,32,256]{4,3,2,1,0:T(8,128)}, u32[]{:S(2)}, u32[]{:S(2)}) collective-permute-start(f32[2,22,1,32,256]{4,3,2,1,0:T(8,128)} %get-tuple-element.36), channel_id=1, source_target_pairs={{1,0},{2,1},{3,2},{4,3},{5,4},{6,5},{7,6},{8,7},{9,8},{10,9},{11,1... | collective-permute-start | bytes 4325384 | tf_op jit(solution)/shard_map/ppermute | solution.py:24
  351.2 11.3 %fusion.66 = (f32[2,22,4,31,256]{4,3,2,1,0:T(8,128)}, f32[2,22,4,31,256]{4,3,2,1,0:T(8,128)}) fusion(f32[2,22,4,32,256]{4,3,2,1,0:T(8,128)} %copy-done.1), kind=kLoop, calls=%fused_computation.147 | loop fusion | bytes 22347776 | tf_op jit(solution)/shard_map/jit(_roll_static)/slice | solution.py:33
  362.6 6.4 %fusion.68 = (f32[2,22,4,32,255]{4,3,2,1,0:T(8,128)}, f32[2,22,4,32,255]{4,3,2,1,0:T(8,128)}) fusion(f32[2,22,4,32,256]{4,3,2,1,0:T(8,128)S(1)} %copy-done.2), kind=kLoop, calls=%fused_computation.149 | loop fusion | bytes 22978560 | tf_op jit(solution)/shard_map/jit(_roll_static)/slice | solution.py:34
  369.0 12.1 %collective-permute-done.6 = f32[2,22,1,32,256]{4,3,2,1,0:T(8,128)} collective-permute-done((f32[2,22,1,32,256]{4,3,2,1,0:T(8,128)}, f32[2,22,1,32,256]{4,3,2,1,0:T(8,128)}, u32[]{:S(2)}, u32[]{:S(2)}) %collective-permute-start.6) | collective-permute-done | bytes 1441824 | tf_op jit(solution)/shard_map/ppermute | solution.py:23
  381.0 17.4 %fusion.62 = (f32[22,4,32,256]{3,2,1,0:T(8,128)}, f32[2,22,4,32,256]{4,3,2,1,0:T(8,128)}) fusion(f32[2,4,32,256]{3,2,1,0:T(8,128)} %get-tuple-element.93, f32[2,4,32,256]{3,2,1,0:T(8,128)} %get-tuple-element.94, f32[2,4,32,256]{3,2,1,0:T(8,128)S(1)} %copy-done.13, f32[2,22,4,32,256]{4,3,2,1,0:T(8,128)S(1)} %copy-done.2, f32[4,32,256]{2,1,0:T(8,128)S(1)} %copy-done.5, ...), kind=kLoop, calls=%fused_computation.143 | loop fusion | flops 64159744 | bytes 41943040 | tf_op jit(solution)/shard_map/reduce_sum | solution.py:92
  398.5 73.4 %all-reduce.9.cloned.1.call-done = f32[22,4,32,256]{3,2,1,0:T(8,128)} async-done(((f32[22,4,32,256]{3,2,1,0:T(8,128)}), f32[22,4,32,256]{3,2,1,0:T(8,128)}) %all-reduce.9.cloned.1.call-update) | async-done | bytes 2883600 | tf_op jit(solution)/shard_map/psum | solution.py:92
  474.1 6.2 %gather_fusion.2 = f32[1024]{0:T(1024)S(1)} fusion(f32[32768]{0:T(1024)S(1)} %bitcast.65, s32[1024]{0:T(1024)S(1)} %broadcast_clamp_fusion), kind=kCustom, calls=%fused_computation.2 | custom fusion | bytes 12288 | tf_op jit(solution)/shard_map/gather | solution.py:94
  480.3 6.2 %gather_fusion.3 = f32[1024]{0:T(1024)S(1)} fusion(f32[32768]{0:T(1024)S(1)} %bitcast.64, s32[1024]{0:T(1024)S(1)} %broadcast_clamp_fusion), kind=kCustom, calls=%fused_computation.3 | custom fusion | bytes 12288 | tf_op jit(solution)/shard_map/gather | solution.py:95
  487.2 6.1 %scatter_custom_fusion.3 = f32[32768]{0:T(1024)S(1)} fusion(s32[1024]{0:T(1024)} %bitcast.82, f32[1024]{0:T(1024)S(1)} %bitcast.79, f32[]{:T(128)} %constant.72.clone.1), kind=kCustom, calls=%fused_computation.122 | custom fusion | flops 1024 | bytes 131584 | tf_op jit(solution)/shard_map/scatter-add | solution.py:77
  493.3 6.1 %scatter_custom_fusion.2 = f32[32768]{0:T(1024)S(1)} fusion(s32[1024]{0:T(1024)} %bitcast.83, f32[1024]{0:T(1024)S(1)} %bitcast.74, f32[]{:T(128)} %constant.72.clone.1), kind=kCustom, calls=%fused_computation.124 | custom fusion | flops 1024 | bytes 131584 | tf_op jit(solution)/shard_map/scatter-add | solution.py:76
  500.2 6.5 %multiply_subtract_fusion = f32[2,22,4,32,256]{4,3,2,1,0:T(8,128)} fusion(f32[2,22,4,32,256]{4,3,2,1,0:T(8,128)} %get-tuple-element.30, f32[22,4,32,256]{3,2,1,0:T(8,128)S(1)} %broadcast_multiply_fusion, f32[4,32,256]{2,1,0:T(8,128)S(1)} %copy-done.12), kind=kLoop, calls=%fused_computation.32 | loop fusion | flops 4325376 | bytes 14548992 | tf_op jit(solution)/shard_map/sub | solution.py:68
  506.8 33.6 %all-reduce.11.cloned.1.call-done = f32[2,4,32,256]{3,2,1,0:T(8,128)} async-done(((f32[2,4,32,256]{3,2,1,0:T(8,128)}), f32[2,4,32,256]{3,2,1,0:T(8,128)}) %all-reduce.11.cloned.1.call-update) | async-done | bytes 262160 | tf_op jit(solution)/shard_map/psum | solution.py:98
  (100 shorter events, 66.2 us)
Async XLA Ops:
  7.2 193.3 %all-reduce.5.cloned.1.call-start = ((), (), s32[]{:S(2)}) async-start(), calls=%async_computation | async-start | bytes 5767168 | tf_op jit(solution)/shard_map/psum | solution.py:92
  7.2 11.8 %copy-start.3 = (f32[2,22,4,32,256]{4,3,2,1,0:T(8,128)S(1)}, f32[2,22,4,32,256]{4,3,2,1,0:T(8,128)}, u32[]{:S(2)}) copy-start(f32[2,22,4,32,256]{4,3,2,1,0:T(8,128)} %param.11) | copy-start | bytes 17301508
  11.2 39.4 %collective-permute-start = (f32[2,22,1,32,256]{4,3,2,1,0:T(8,128)}, f32[2,22,1,32,256]{4,3,2,1,0:T(8,128)}, u32[]{:S(2)}, u32[]{:S(2)}) collective-permute-start(f32[2,22,1,32,256]{4,3,2,1,0:T(8,128)} %get-tuple-element.65), channel_id=1, source_target_pairs={{0,1},{1,2},{2,3},{3,4},{4,5},{5,6},{6,7},{7,8},{8,9},{9,10},{10,1... | collective-permute-start | bytes 4325384 | tf_op jit(solution)/shard_map/ppermute | solution.py:23
  13.6 8.9 %copy-start.10 = (s32[2,2,2,3,4,32,256]{6,5,4,3,2,1,0:T(8,128)S(1)}, s32[2,2,2,3,4,32,256]{6,5,4,3,2,1,0:T(8,128)}, u32[]{:S(2)}) copy-start(s32[2,2,2,3,4,32,256]{6,5,4,3,2,1,0:T(8,128)} %param.13) | copy-start | bytes 9437188
  13.6 37.0 %collective-permute-start.1 = (f32[2,22,1,32,256]{4,3,2,1,0:T(8,128)}, f32[2,22,1,32,256]{4,3,2,1,0:T(8,128)}, u32[]{:S(2)}, u32[]{:S(2)}) collective-permute-start(f32[2,22,1,32,256]{4,3,2,1,0:T(8,128)} %get-tuple-element.66), channel_id=1, source_target_pairs={{1,0},{2,1},{3,2},{4,3},{5,4},{6,5},{7,6},{8,7},{9,8},{10,9},{11,1... | collective-permute-start | bytes 4325384 | tf_op jit(solution)/shard_map/ppermute | solution.py:24
  21.6 4.2 copy-start.15
  25.9 82.5 %copy-start.4 = (f32[4,32,256]{2,1,0:T(8,128)}, f32[4,32,256]{2,1,0:T(8,128)S(1)}, u32[]{:S(2)}) copy-start(f32[4,32,256]{2,1,0:T(8,128)S(1)} %get-tuple-element.98) | copy-start | bytes 393220
  25.9 82.4 %copy-start.6 = (f32[4,32,256]{2,1,0:T(8,128)}, f32[4,32,256]{2,1,0:T(8,128)S(1)}, u32[]{:S(2)}) copy-start(f32[4,32,256]{2,1,0:T(8,128)S(1)} %get-tuple-element.99) | copy-start | bytes 393220
  25.9 82.4 %copy-start.8 = (f32[4,32,256]{2,1,0:T(8,128)}, f32[4,32,256]{2,1,0:T(8,128)S(1)}, u32[]{:S(2)}) copy-start(f32[4,32,256]{2,1,0:T(8,128)S(1)} %get-tuple-element.100) | copy-start | bytes 393220
  72.0 36.4 %collective-permute-start.2 = (f32[2,22,1,32,256]{4,3,2,1,0:T(8,128)}, f32[2,22,1,32,256]{4,3,2,1,0:T(8,128)}, u32[]{:S(2)}, u32[]{:S(2)}) collective-permute-start(f32[2,22,1,32,256]{4,3,2,1,0:T(8,128)} %get-tuple-element.55), channel_id=1, source_target_pairs={{0,1},{1,2},{2,3},{3,4},{4,5},{5,6},{6,7},{7,8},{8,9},{9,10},{10,1... | collective-permute-start | bytes 4325384 | tf_op jit(solution)/shard_map/ppermute | solution.py:23
  72.0 36.4 %collective-permute-start.3 = (f32[2,22,1,32,256]{4,3,2,1,0:T(8,128)}, f32[2,22,1,32,256]{4,3,2,1,0:T(8,128)}, u32[]{:S(2)}, u32[]{:S(2)}) collective-permute-start(f32[2,22,1,32,256]{4,3,2,1,0:T(8,128)} %get-tuple-element.56), channel_id=1, source_target_pairs={{1,0},{2,1},{3,2},{4,3},{5,4},{6,5},{7,6},{8,7},{9,8},{10,9},{11,1... | collective-permute-start | bytes 4325384 | tf_op jit(solution)/shard_map/ppermute | solution.py:24
  108.4 17.6 %copy-start.19 = (s32[1,1024]{1,0:T(1,128)S(1)}, s32[1,1024]{1,0:T(1,128)}, u32[]{:S(2)}) copy-start(s32[1,1024]{1,0:T(1,128)} %param.15) | copy-start | bytes 12292
  125.9 150.5 %all-reduce.7.cloned.1.call-start = ((), (), s32[]{:S(2)}) async-start(), calls=%async_computation.1 | async-start | bytes 524288 | tf_op jit(solution)/shard_map/psum | solution.py:98
  202.6 16.9 %copy-start.16 = (f32[1,1024]{1,0:T(1,128)S(1)}, f32[1,1024]{1,0:T(1,128)}, u32[]{:S(2)}) copy-start(f32[1,1024]{1,0:T(1,128)} %param.16) | copy-start | bytes 12292
  202.6 16.9 %copy-start.17 = (f32[1,1024]{1,0:T(1,128)S(1)}, f32[1,1024]{1,0:T(1,128)}, u32[]{:S(2)}) copy-start(f32[1,1024]{1,0:T(1,128)} %param.17) | copy-start | bytes 12292
  213.3 23.1 %copy-start.11 = (f32[4,32,256]{2,1,0:T(8,128)S(1)}, f32[4,32,256]{2,1,0:T(8,128)}, u32[]{:S(2)}) copy-start(f32[4,32,256]{2,1,0:T(8,128)} %broadcast_multiply_fusion.4) | copy-start | bytes 393220
  236.2 235.7 %all-reduce.9.cloned.1.call-start = ((), (), s32[]{:S(2)}) async-start(), calls=%async_computation.2 | async-start | bytes 5767168 | tf_op jit(solution)/shard_map/psum | solution.py:92
  279.3 5.5 %copy-start = (f32[2,22,4,32,256]{4,3,2,1,0:T(8,128)S(1)}, f32[2,22,4,32,256]{4,3,2,1,0:T(8,128)}, u32[]{:S(2)}) copy-start(f32[2,22,4,32,256]{4,3,2,1,0:T(8,128)} %fusion.29) | copy-start | bytes 17301508
  286.7 37.6 %collective-permute-start.4 = (f32[2,22,1,32,256]{4,3,2,1,0:T(8,128)}, f32[2,22,1,32,256]{4,3,2,1,0:T(8,128)}, u32[]{:S(2)}, u32[]{:S(2)}) collective-permute-start(f32[2,22,1,32,256]{4,3,2,1,0:T(8,128)} %get-tuple-element.45), channel_id=1, source_target_pairs={{0,1},{1,2},{2,3},{3,4},{4,5},{5,6},{6,7},{7,8},{8,9},{9,10},{10,1... | collective-permute-start | bytes 4325384 | tf_op jit(solution)/shard_map/ppermute | solution.py:23
  287.9 36.3 %collective-permute-start.5 = (f32[2,22,1,32,256]{4,3,2,1,0:T(8,128)}, f32[2,22,1,32,256]{4,3,2,1,0:T(8,128)}, u32[]{:S(2)}, u32[]{:S(2)}) collective-permute-start(f32[2,22,1,32,256]{4,3,2,1,0:T(8,128)} %get-tuple-element.46), channel_id=1, source_target_pairs={{1,0},{2,1},{3,2},{4,3},{5,4},{6,5},{7,6},{8,7},{9,8},{10,9},{11,1... | collective-permute-start | bytes 4325384 | tf_op jit(solution)/shard_map/ppermute | solution.py:24
  299.0 25.2 %copy-start.5 = (f32[4,32,256]{2,1,0:T(8,128)S(1)}, f32[4,32,256]{2,1,0:T(8,128)}, u32[]{:S(2)}) copy-start(f32[4,32,256]{2,1,0:T(8,128)} %copy-done.4) | copy-start | bytes 393220
  299.0 25.2 %copy-start.7 = (f32[4,32,256]{2,1,0:T(8,128)S(1)}, f32[4,32,256]{2,1,0:T(8,128)}, u32[]{:S(2)}) copy-start(f32[4,32,256]{2,1,0:T(8,128)} %copy-done.6) | copy-start | bytes 393220
  299.0 25.2 %copy-start.9 = (f32[4,32,256]{2,1,0:T(8,128)S(1)}, f32[4,32,256]{2,1,0:T(8,128)}, u32[]{:S(2)}) copy-start(f32[4,32,256]{2,1,0:T(8,128)} %copy-done.8) | copy-start | bytes 393220
  299.0 25.2 %copy-start.14 = (f32[2,4,32,256]{3,2,1,0:T(8,128)S(1)}, f32[2,4,32,256]{3,2,1,0:T(8,128)}, u32[]{:S(2)}) copy-start(f32[2,4,32,256]{3,2,1,0:T(8,128)} %get-tuple-element.83) | copy-start | bytes 786436
  339.4 10.9 %copy-start.1 = (f32[2,22,4,32,256]{4,3,2,1,0:T(8,128)}, f32[2,22,4,32,256]{4,3,2,1,0:T(8,128)S(1)}, u32[]{:S(2)}) copy-start(f32[2,22,4,32,256]{4,3,2,1,0:T(8,128)S(1)} %multiply_add_fusion.1) | copy-start | bytes 17301508
  344.4 36.6 %collective-permute-start.6 = (f32[2,22,1,32,256]{4,3,2,1,0:T(8,128)}, f32[2,22,1,32,256]{4,3,2,1,0:T(8,128)}, u32[]{:S(2)}, u32[]{:S(2)}) collective-permute-start(f32[2,22,1,32,256]{4,3,2,1,0:T(8,128)} %get-tuple-element.35), channel_id=1, source_target_pairs={{0,1},{1,2},{2,3},{3,4},{4,5},{5,6},{6,7},{7,8},{8,9},{9,10},{10,1... | collective-permute-start | bytes 4325384 | tf_op jit(solution)/shard_map/ppermute | solution.py:23
  344.4 36.6 %collective-permute-start.7 = (f32[2,22,1,32,256]{4,3,2,1,0:T(8,128)}, f32[2,22,1,32,256]{4,3,2,1,0:T(8,128)}, u32[]{:S(2)}, u32[]{:S(2)}) collective-permute-start(f32[2,22,1,32,256]{4,3,2,1,0:T(8,128)} %get-tuple-element.36), channel_id=1, source_target_pairs={{1,0},{2,1},{3,2},{4,3},{5,4},{6,5},{7,6},{8,7},{9,8},{10,9},{11,1... | collective-permute-start | bytes 4325384 | tf_op jit(solution)/shard_map/ppermute | solution.py:24
  351.2 11.3 %copy-start.2 = (f32[2,22,4,32,256]{4,3,2,1,0:T(8,128)S(1)}, f32[2,22,4,32,256]{4,3,2,1,0:T(8,128)}, u32[]{:S(2)}) copy-start(f32[2,22,4,32,256]{4,3,2,1,0:T(8,128)} %copy-done.1) | copy-start | bytes 17301508
  362.6 18.5 %copy-start.13 = (f32[2,4,32,256]{3,2,1,0:T(8,128)S(1)}, f32[2,4,32,256]{3,2,1,0:T(8,128)}, u32[]{:S(2)}) copy-start(f32[2,4,32,256]{3,2,1,0:T(8,128)} %get-tuple-element.92) | copy-start | bytes 786436
  398.5 142.0 %all-reduce.11.cloned.1.call-start = ((), (), s32[]{:S(2)}) async-start(), calls=%async_computation.3 | async-start | bytes 524288 | tf_op jit(solution)/shard_map/psum | solution.py:98
  474.0 12.5 %copy-start.18 = (f32[1,1024]{1,0:T(1,128)S(1)}, f32[1,1024]{1,0:T(1,128)}, u32[]{:S(2)}) copy-start(f32[1,1024]{1,0:T(1,128)} %get-tuple-element.32) | copy-start | bytes 12292
  474.0 26.3 %copy-start.12 = (f32[4,32,256]{2,1,0:T(8,128)S(1)}, f32[4,32,256]{2,1,0:T(8,128)}, u32[]{:S(2)}) copy-start(f32[4,32,256]{2,1,0:T(8,128)} %broadcast_multiply_fusion.4) | copy-start | bytes 393220
Sparse Core Ops, SparseCore 0:
  126.0 74.4 all-reduce.4
  236.3 40.0 all-reduce.6
  398.6 73.2 all-reduce.8
  500.4 40.0 all-reduce.10
where the time goes:
time: 558 us; the launch traced here: 550 us
  waiting for transfers between devices  270 us (48%)
  other arithmetic  126 us (23%)
  local copies, waits for them, and re-layouts  114 us (20%)
  starting transfers between devices  25.6 us (5%)
  between operations  14.6 us (3%)
    psum x2, waiting for transfers between devices, on_device(): total = lax.psum(jnp.sum(fields, axis=0), 'field')  142 us
    psum x2, waiting for transfers between devices, on_device(): sources = lax.psum(local_sources, 'field')  67 us
    ppermute x4, waiting for transfers between devices, with_halo(): before = lax.ppermute(last, axis, up)  61 us
    slice x8, local copies, waits for them, and re-layouts, advance(): jnp.roll(center, 1, 4)  39.4 us
    reduce_sum x2, other arithmetic, on_device(): total = lax.psum(jnp.sum(fields, axis=0), 'field')  34.9 us
    slice x8, local copies, waits for them, and re-layouts, advance(): jnp.roll(center, 1, 3)  32.3 us
    add x2, other arithmetic, advance(): center + sub_time * (diffusivity * spread - advect) + noise_gain * stirred  32.1 us
    ppermute x4, starting transfers between devices, with_halo(): after = lax.ppermute(first, axis, down)  21.5 us
  transfers between devices with their start and end apart: 12, of which 8 were waited for; matrix products, arithmetic and copies ran while one was open for 15% of the time, Pallas kernels for 0%

commit v1 on v0

v1 whole, which is shorter than its diff:
```python
import jax
import jax.numpy as jnp
from jax import lax
from jax.experimental import pallas as pl
from jax.experimental.pallas import tpu as pltpu
from jax.sharding import PartitionSpec as P

MESH = pl.DeviceIdType.MESH
F32 = jnp.float32
BF16 = jnp.bfloat16

S, CX, NY, NZ = 22, 4, 32, 256
CHUNKS = S // 2
GROUPS, P_DEV = 4, 1024
ROWS = CX * NY
P_BLOCK = 512

sub_time = 0.2
diffusivity = 0.1
noise_gain = 0.2
step_time = 0.4
latent_heat = 0.5

LAG_TOTAL = 3
LAG_RELAX = 4


def split3(value):
    top = value.astype(BF16)
    rest = value - top.astype(F32)
    middle = rest.astype(BF16)
    return top, middle, (rest - middle.astype(F32)).astype(BF16)


def kernel(
    fields_in, velocity_in, noise_in, mixing_in, cell_in, mass_in, temp_in,
    fields_out, mass_out, temp_out,
    old, new, halo, noise, velocity, weight, coef, coef_mid,
    part, part_land, pair, pair_land, mean, source,
    cells, masses, temps,
    load_sem, parcel_load_sem, halo_send, halo_recv, mean_send, mean_recv,
    parcel_send, parcel_recv, out_sem,
):
    f = lax.axis_index("field")
    s = lax.axis_index("space")
    blocks = lax.axis_size("space")
    core = lax.rem(f, 2)
    above = {"space": lax.rem(s + 1, blocks)}
    below = {"space": lax.rem(s + blocks - 1, blocks)}
    twin = {"field": f + 1 - 2 * core}
    across = {"field": lax.rem(f + 2, 4)}
    corner = {"field": 3 - f}

    loads = [
        pltpu.make_async_copy(velocity_in, velocity, load_sem.at[0]),
        pltpu.make_async_copy(noise_in, noise, load_sem.at[1]),
        pltpu.make_async_copy(fields_in, old, load_sem.at[2]),
        pltpu.make_async_copy(mixing_in, weight, load_sem.at[3]),
    ]
    for load in loads:
        load.start()
    parcel_loads = [
        pltpu.make_async_copy(array, held.at[f], parcel_load_sem.at[k])
        for k, (array, held) in enumerate(((cell_in, cells), (mass_in, masses), (temp_in, temps)))
    ]
    for load in parcel_loads:
        load.start()

    barrier = pltpu.get_barrier_semaphore()
    for peer in (above, below, twin, across, corner):
        pl.semaphore_signal(barrier, 1, device_id=peer, device_id_type=MESH)
    pl.semaphore_wait(barrier, 5)

    def halo_copy(phase, side, c):
        plane = CX - 1 if side == 0 else 0
        held = (fields_in, new, old, new)[phase]
        return pltpu.make_async_remote_copy(
            src_ref=held.at[:, pl.ds(2 * c, 2), plane],
            dst_ref=halo.at[phase, side, :, pl.ds(2 * c, 2)],
            send_sem=halo_send.at[phase, side, c],
            recv_sem=halo_recv.at[phase, side, c],
            device_id=above if side == 0 else below,
            device_id_type=MESH,
        )

    def send_halo(phase, c):
        for side in range(2):
            halo_copy(phase, side, c).start()

    def mean_copy(step, stage, c):
        src, dst, peer = (
            (part.at[step, 2 * c + 1 - core], part_land.at[step, c], twin),
            (pair.at[step, c], pair_land.at[step, c], across),
            (mean.at[step, 2 * c + core], mean.at[step, 2 * c + core], twin),
        )[stage]
        return pltpu.make_async_remote_copy(
            src_ref=src, dst_ref=dst,
            send_sem=mean_send.at[step, stage, c], recv_sem=mean_recv.at[step, stage, c],
            device_id=peer, device_id_type=MESH,
        )

    def start_halo(c, carry):
        send_halo(0, c)
        return carry

    lax.fori_loop(0, CHUNKS, start_halo, 0)

    for load in parcel_loads:
        load.wait()
    parcel_copies = [
        pltpu.make_async_remote_copy(
            src_ref=held.at[f], dst_ref=held.at[f],
            send_sem=parcel_send.at[k, i], recv_sem=parcel_recv.at[k, i],
            device_id=peer, device_id_type=MESH,
        )
        for k, held in enumerate((cells, masses, temps))
        for i, peer in enumerate((twin, across, corner))
    ]
    for copy in parcel_copies:
        copy.start()

    def set_coef(step, sub_step):
        def one(b, carry):
            for p in range(CX):
                for d in range(3):
                    speed = velocity[d, p]
                    drift = (0.5 * noise_gain) * noise[step, sub_step, b, d, p].astype(F32)
                    coef[b, p, 2 * d] = (sub_time * diffusivity) + sub_time * jnp.maximum(speed, 0.0) - drift
                    coef[b, p, 2 * d + 1] = (sub_time * diffusivity) - sub_time * jnp.minimum(speed, 0.0) + drift
            return carry

        lax.fori_loop(0, 2, one, 0)

    loads[0].wait()
    for p in range(CX):
        speeds = jnp.abs(velocity[0, p]) + jnp.abs(velocity[1, p]) + jnp.abs(velocity[2, p])
        coef_mid[p] = (1.0 - 6.0 * sub_time * diffusivity) - sub_time * speeds
    loads[1].wait()
    set_coef(0, 0)
    loads[2].wait()
    loads[3].wait()
    weight[...] = step_time * weight[...]

    def substep(phase, c):
        held, made = ((old, new), (new, old))[phase % 2]

        def one(b, carry):
            for p in range(CX):
                for j in range(2):
                    n = 2 * c + j
                    q = held[b, n, p]
                    lower = held[b, n, p - 1] if p else halo[phase, 0, b, n]
                    upper = held[b, n, p + 1] if p < CX - 1 else halo[phase, 1, b, n]
                    made[b, n, p] = (
                        coef_mid[p] * q
                        + coef[b, p, 0] * lower
                        + coef[b, p, 1] * upper
                        + coef[b, p, 2] * pltpu.roll(q, 1, 0)
                        + coef[b, p, 3] * pltpu.roll(q, NY - 1, 0)
                        + coef[b, p, 4] * pltpu.roll(q, 1, 1)
                        + coef[b, p, 5] * pltpu.roll(q, NZ - 1, 1)
                    )
            return carry

        lax.fori_loop(0, 2, one, 0)

    def evaporate(step):
        stacked = jnp.concatenate(
            [piece for n in range(2) for piece in split3(mean[step, n].reshape(ROWS, NZ))], axis=0
        )
        source[...] = jnp.zeros_like(source)
        per_group = P_DEV // P_BLOCK

        def one(i, carry):
            g = i // per_group
            at = pl.ds(pl.multiple_of(lax.rem(i, per_group) * P_BLOCK, P_BLOCK), P_BLOCK)
            cell = cells[g, :, at]
            in_row = lax.shift_right_logical(cell, 8) == lax.broadcasted_iota(jnp.int32, (ROWS, P_BLOCK), 0)
            in_column = jnp.where(
                (cell & (NZ - 1)) == lax.broadcasted_iota(jnp.int32, (NZ, P_BLOCK), 0), 1.0, 0.0
            ).astype(BF16)
            picked = jnp.dot(stacked, in_column, preferred_element_type=F32)

            def of(n):
                piece = [picked[(3 * n + k) * ROWS:(3 * n + k + 1) * ROWS] for k in range(3)]
                return jnp.sum(jnp.where(in_row, piece[0] + piece[1] + piece[2], 0.0), axis=0, keepdims=True)

            vapor, gas_heat = of(0), of(1)
            mass, temper = masses[g, :, at], temps[g, :, at]
            sat = 0.8 / (1.0 + jnp.exp(-4.0 * (temper - 1.0)))
            drive = jnp.maximum(sat - vapor, 0.0) / (1.0 - sat)
            rate = mass * jnp.log1p(drive)
            heat = rate * (gas_heat - latent_heat)
            masses[g, :, at] = mass - step_time * rate
            temps[g, :, at] = temper + step_time * (gas_heat - temper)
            spread = jnp.concatenate(
                [
                    jnp.where(in_row, piece.astype(F32), 0.0).astype(BF16)
                    for value in (rate, heat)
                    for piece in split3(value)
                ],
                axis=0,
            )
            summed = lax.dot_general(
                spread, in_column, (((1,), (1,)), ((), ())), preferred_element_type=F32
            )
            for n in range(2):
                piece = [summed[(3 * n + k) * ROWS:(3 * n + k + 1) * ROWS] for k in range(3)]
                source[n] += piece[0] + piece[1] + piece[2]
            return carry

        lax.fori_loop(0, GROUPS * per_group, one, 0)

    def sum_parts(step, c):
        def one(p, carry):
            for j in range(2):
                part[step, 2 * c + j, p] = old[0, 2 * c + j, p] + old[1, 2 * c + j, p]
            return carry

        lax.fori_loop(0, CX, one, 0)

    def relax(step, c):
        def one(p, carry):
            for j in range(2):
                for b in range(2):
                    moved = old[b, 2 * c + j, p]
                    old[b, 2 * c + j, p] = moved - weight[p] * (moved - mean[step, 2 * c + j, p])
            return carry

        lax.fori_loop(0, CX, one, 0)

        @pl.when(c == 0)
        def _():
            if step == 0:
                for copy in parcel_copies:
                    copy.wait()
            evaporate(step)
            for j in range(2):
                for p in range(CX):
                    for b in range(2):
                        old[b, j, p] += step_time * source[j, p * NY:(p + 1) * NY]

    def out_copy(c):
        at = pl.ds(2 * c, 2)
        return pltpu.make_async_copy(old.at[:, at], fields_out.at[:, at], out_sem.at[c])

    for step in range(2):
        if step:
            set_coef(step, 0)

        def first(c, carry):
            for side in range(2):
                halo_copy(2 * step, side, c).wait_recv()
                if step:
                    halo_copy(1, side, c).wait_send()
            substep(2 * step, c)
            send_halo(2 * step + 1, c)
            return carry

        lax.fori_loop(0, CHUNKS, first, 0)
        set_coef(step, 1)

        def second(i, carry):
            @pl.when(i < CHUNKS)
            def _():
                c = i
                for side in range(2):
                    halo_copy(2 * step + 1, side, c).wait_recv()
                    if step:
                        halo_copy(2, side, c).wait_send()
                substep(2 * step + 1, c)
                sum_parts(step, c)
                mean_copy(step, 0, c).start()

            @pl.when((i >= 1) & (i < CHUNKS + 1))
            def _():
                c = i - 1
                mean_copy(step, 0, c).wait_recv()
                pair[step, c] = part[step, 2 * c + core] + part_land[step, c]
                mean_copy(step, 1, c).start()

            @pl.when((i >= LAG_TOTAL) & (i < CHUNKS + LAG_TOTAL))
            def _():
                c = i - LAG_TOTAL
                mean_copy(step, 1, c).wait_recv()
                mean[step, 2 * c + core] = 0.125 * (pair[step, c] + pair_land[step, c])
                mean_copy(step, 2, c).start()

            @pl.when(i >= LAG_RELAX)
            def _():
                c = i - LAG_RELAX
                mean_copy(step, 2, c).wait_recv()
                relax(step, c)
                if step == 0:
                    send_halo(2, c)
                else:
                    out_copy(c).start()

            return carry

        lax.fori_loop(0, CHUNKS + LAG_RELAX, second, 0)

    mass_out[...] = masses[f]
    temp_out[...] = temps[f]

    def finish(c, carry):
        for side in range(2):
            halo_copy(0, side, c).wait_send()
            halo_copy(3, side, c).wait_send()
        for step in range(2):
            for stage in range(3):
                mean_copy(step, stage, c).wait_send()
        out_copy(c).wait()
        return carry

    lax.fori_loop(0, CHUNKS, finish, 0)


def on_device(fields, velocity, noise, mixing_rate, parcel_cell, parcel_mass, parcel_temp):
    anywhere = pl.BlockSpec(memory_space=pl.ANY)
    in_vmem = pl.BlockSpec(memory_space=pltpu.VMEM)
    plane = (NY, NZ)
    block = (CX,) + plane
    dma = pltpu.SemaphoreType.DMA
    return pl.pallas_call(
        kernel,
        out_shape=(
            jax.ShapeDtypeStruct(fields.shape, F32),
            jax.ShapeDtypeStruct(parcel_mass.shape, F32),
            jax.ShapeDtypeStruct(parcel_temp.shape, F32),
        ),
        in_specs=[anywhere] * 7,
        out_specs=(anywhere, in_vmem, in_vmem),
        scratch_shapes=[
            pltpu.VMEM((2, S) + block, F32),
            pltpu.VMEM((2, S) + block, F32),
            pltpu.VMEM((4, 2, 2, S) + plane, F32),
            pltpu.VMEM(noise.shape, jnp.int32),
            pltpu.VMEM((3,) + block, F32),
            pltpu.VMEM(block, F32),
            pltpu.VMEM((2, CX, 6) + plane, F32),
            pltpu.VMEM(block, F32),
            pltpu.VMEM((2, S) + block, F32),
            pltpu.VMEM((2, CHUNKS) + block, F32),
            pltpu.VMEM((2, CHUNKS) + block, F32),
            pltpu.VMEM((2, CHUNKS) + block, F32),
            pltpu.VMEM((2, S) + block, F32),
            pltpu.VMEM((2, ROWS, NZ), F32),
            pltpu.VMEM((GROUPS, 1, P_DEV), jnp.int32),
            pltpu.VMEM((GROUPS, 1, P_DEV), F32),
            pltpu.VMEM((GROUPS, 1, P_DEV), F32),
            dma((4,)),
            dma((3,)),
            dma((4, 2, CHUNKS)),
            dma((4, 2, CHUNKS)),
            dma((2, 3, CHUNKS)),
            dma((2, 3, CHUNKS)),
            dma((3, 3)),
            dma((3, 3)),
            dma((CHUNKS,)),
        ],
        compiler_params=pltpu.CompilerParams(
            collective_id=0, has_side_effects=True, vmem_limit_bytes=62 << 20
        ),
    )(fields, velocity, noise, mixing_rate, parcel_cell, parcel_mass, parcel_temp)


def solution(mesh):
    placed = (
        P("field", None, "space", None, None),
        P(None, "space", None, None),
        P(None, None, "field", None, "space", None, None),
        P("space", None, None),
        P("field", "space"),
        P("field", "space"),
        P("field", "space"),
    )
    return jax.shard_map(
        on_device,
        mesh=mesh,
        in_specs=placed,
        out_specs=(P("field", None, "space", None, None), P("field", "space"), P("field", "space")),
        check_vma=False,
    )
```

time: 558 us -> 236 us (0.42)
  the two profiles are of different devices: /device:TPU:1 before, /device:TPU:3 now
where the time goes in v1:
time: 236 us
  Pallas kernels  228 us (97%)
  local copies, waits for them, and re-layouts  7.35 us (3%)
    pallas_call x1, Pallas kernels, on_device(): pl.pallas_call(kernel, out_shape=(jax.ShapeDtypeStruct(fields.shape, F32)...  228 us
    unnamed x7, local copies, waits for them, and re-layouts  7.35 us

profile of v1, /device:TPU:3, one launch (start us, length us, event | category | flops | bytes accessed | tf_op | source)
XLA Modules:
  0.0 236.2 jit_solution(10342326343192692046)
XLA Ops:
  0.6 228.2 %shard_map.94 = (f32[2,22,4,32,256]{4,3,2,1,0:T(8,128)}, f32[1,1024]{1,0:T(1,128)}, f32[1,1024]{1,0:T(1,128)}) custom-call(f32[2,22,4,32,256]{4,3,2,1,0:T(8,128)} %fields_in.1, f32[3,4,32,256]{3,2,1,0:T(8,128)} %velocity_in.1, s32[2,2,2,3,4,32,256]{6,5,4,3,2,1,0:T(8,128)} %noise_in.1, f32[4,32,256]{2,1,0:T(8,128)} %mixing_in.1, s32[1,1024]{1,0:T(1,128)} %cell_in.1, ...), custom_call_target="tpu_custom_call" | custom-call | tf_op jit(solution)/shard_map/pallas_call | solution.py:325
  228.8 0.0 copy-start.1
  228.8 0.0 copy-start
  228.8 6.2 %copy.13 = f32[2,22,4,32,256]{4,3,2,1,0:T(8,128)} copy(f32[2,22,4,32,256]{4,3,2,1,0:T(8,128)} %get-tuple-element.6) | data formatting | bytes 11534336
  235.0 0.0 copy-done.1
  235.0 0.6 copy.14
  235.6 0.0 copy-done
  235.6 0.6 copy.15
Async XLA Ops:
  228.8 6.2 %copy-start.1 = (f32[1,1024]{1,0:T(1,128)S(1)}, f32[1,1024]{1,0:T(1,128)}, u32[]{:S(2)}) copy-start(f32[1,1024]{1,0:T(1,128)} %get-tuple-element.7) | copy-start | bytes 12292
  228.8 6.8 %copy-start = (f32[1,1024]{1,0:T(1,128)S(1)}, f32[1,1024]{1,0:T(1,128)}, u32[]{:S(2)}) copy-start(f32[1,1024]{1,0:T(1,128)} %get-tuple-element.8) | copy-start | bytes 12292

commit v2 on v1

--- a/solution.py
+++ b/solution.py
@@ -23,6 +23,7 @@
 
 LAG_TOTAL = 3
 LAG_RELAX = 4
+LAG_PASS = 4
 
 
 def split3(value):
@@ -34,12 +35,12 @@
 
 def kernel(
     fields_in, velocity_in, noise_in, mixing_in, cell_in, mass_in, temp_in,
-    fields_out, mass_out, temp_out,
-    old, new, halo, noise, velocity, weight, coef, coef_mid,
+    old, mass_out, temp_out,
+    new, halo, noise, velocity, weight, coef, coef_mid,
     part, part_land, pair, pair_land, mean, source,
     cells, masses, temps,
     load_sem, parcel_load_sem, halo_send, halo_recv, mean_send, mean_recv,
-    parcel_send, parcel_recv, out_sem,
+    parcel_send, parcel_recv, relay_send,
 ):
     f = lax.axis_index("field")
     s = lax.axis_index("space")
@@ -66,22 +67,79 @@
     for load in parcel_loads:
         load.start()
 
+    base = s - lax.rem(s, 16)
+    other = 16 - base
+    x = lax.rem(s, 16) // 4
+    upward = lax.rem(s, 4) == 3
+    downward = lax.rem(s, 4) == 0
+    edge = upward | downward
+    rank = jnp.where(upward, x, 3 - x)
+    is_relay = edge & (rank != 0)
+    is_end = edge & (rank == 3)
+    relay_side = jnp.where(upward, 0, 1)
+    relay_dest = {"space": base + jnp.where(upward, 0, 15)}
+    relay_source = {"space": other + jnp.where(upward, 15, 0)}
+
     barrier = pltpu.get_barrier_semaphore()
+
+    def greet(peer):
+        pl.semaphore_signal(barrier, 1, device_id=peer, device_id_type=MESH)
+
     for peer in (above, below, twin, across, corner):
-        pl.semaphore_signal(barrier, 1, device_id=peer, device_id_type=MESH)
-    pl.semaphore_wait(barrier, 5)
+        greet(peer)
+
+    @pl.when(is_relay)
+    def _():
+        greet(relay_source)
+
+    @pl.when(is_end)
+    def _():
+        for column in range(1, 4):
+            greet({"space": base + jnp.where(upward, 4 * (3 - column), 4 * column + 3)})
+
+    pl.semaphore_wait(barrier, 5 + jnp.where(is_relay, 1, 0) + jnp.where(is_end, 3, 0))
 
     def halo_copy(phase, side, c):
         plane = CX - 1 if side == 0 else 0
         held = (fields_in, new, old, new)[phase]
+        land, peer = side, (above if side == 0 else below)["space"]
+        if phase:
+            route = lax.rem(c, 4)
+            by_relay = is_end & (upward if side == 0 else downward) & (route != 0)
+            land = jnp.where(by_relay, 2, side)
+            column = 4 * route + 3 if side == 0 else 4 * (3 - route)
+            peer = jnp.where(by_relay, other + column, peer)
         return pltpu.make_async_remote_copy(
             src_ref=held.at[:, pl.ds(2 * c, 2), plane],
-            dst_ref=halo.at[phase, side, :, pl.ds(2 * c, 2)],
+            dst_ref=halo.at[phase, land, :, pl.ds(2 * c, 2)],
             send_sem=halo_send.at[phase, side, c],
-            recv_sem=halo_recv.at[phase, side, c],
-            device_id=above if side == 0 else below,
+            recv_sem=halo_recv.at[phase, land, c],
+            device_id={"space": peer},
             device_id_type=MESH,
         )
+
+    def halo_arrived(phase, side, c):
+        there = halo.at[phase, side, :, pl.ds(2 * c, 2)]
+        pltpu.make_async_copy(there, there, halo_recv.at[phase, side, c]).wait()
+
+    def relay_copy(phase, c):
+        return pltpu.make_async_remote_copy(
+            src_ref=halo.at[phase, 2, :, pl.ds(2 * c, 2)],
+            dst_ref=halo.at[phase, relay_side, :, pl.ds(2 * c, 2)],
+            send_sem=relay_send.at[phase, c],
+            recv_sem=halo_recv.at[phase, relay_side, c],
+            device_id=relay_dest,
+            device_id_type=MESH,
+        )
+
+    def relays(phase, c):
+        return is_relay & (lax.rem(c, 4) == rank)
+
+    def pass_on(phase, c):
+        @pl.when((c >= 0) & (c < CHUNKS) & relays(phase, c))
+        def _():
+            halo_arrived(phase, 2, c)
+            relay_copy(phase, c).start()
 
     def send_halo(phase, c):
         for side in range(2):
@@ -240,17 +298,16 @@
                     for b in range(2):
                         old[b, j, p] += step_time * source[j, p * NY:(p + 1) * NY]
 
-    def out_copy(c):
-        at = pl.ds(2 * c, 2)
-        return pltpu.make_async_copy(old.at[:, at], fields_out.at[:, at], out_sem.at[c])
-
     for step in range(2):
         if step:
             set_coef(step, 0)
 
         def first(c, carry):
+            if step:
+                pass_on(2, c + CHUNKS - LAG_PASS)
+            pass_on(2 * step + 1, c - LAG_PASS)
             for side in range(2):
-                halo_copy(2 * step, side, c).wait_recv()
+                halo_arrived(2 * step, side, c)
                 if step:
                     halo_copy(1, side, c).wait_send()
             substep(2 * step, c)
@@ -261,11 +318,15 @@
         set_coef(step, 1)
 
         def second(i, carry):
+            pass_on(2 * step + 1, i + CHUNKS - LAG_PASS)
+            if step == 0:
+                pass_on(2, i - LAG_RELAX - LAG_PASS)
+
             @pl.when(i < CHUNKS)
             def _():
                 c = i
                 for side in range(2):
-                    halo_copy(2 * step + 1, side, c).wait_recv()
+                    halo_arrived(2 * step + 1, side, c)
                     if step:
                         halo_copy(2, side, c).wait_send()
                 substep(2 * step + 1, c)
@@ -293,8 +354,6 @@
                 relax(step, c)
                 if step == 0:
                     send_halo(2, c)
-                else:
-                    out_copy(c).start()
 
             return carry
 
@@ -310,7 +369,11 @@
         for step in range(2):
             for stage in range(3):
                 mean_copy(step, stage, c).wait_send()
-        out_copy(c).wait()
+        for phase in range(1, 4):
+            @pl.when(relays(phase, c))
+            def _():
+                relay_copy(phase, c).wait_send()
+
         return carry
 
     lax.fori_loop(0, CHUNKS, finish, 0)
@@ -325,16 +388,15 @@
     return pl.pallas_call(
         kernel,
         out_shape=(
-            jax.ShapeDtypeStruct(fields.shape, F32),
-            jax.ShapeDtypeStruct(parcel_mass.shape, F32),
-            jax.ShapeDtypeStruct(parcel_temp.shape, F32),
+            pltpu.VMEM(fields.shape, F32),
+            pltpu.VMEM(parcel_mass.shape, F32),
+            pltpu.VMEM(parcel_temp.shape, F32),
         ),
         in_specs=[anywhere] * 7,
-        out_specs=(anywhere, in_vmem, in_vmem),
+        out_specs=(in_vmem,) * 3,
         scratch_shapes=[
             pltpu.VMEM((2, S) + block, F32),
-            pltpu.VMEM((2, S) + block, F32),
-            pltpu.VMEM((4, 2, 2, S) + plane, F32),
+            pltpu.VMEM((4, 3, 2, S) + plane, F32),
             pltpu.VMEM(noise.shape, jnp.int32),
             pltpu.VMEM((3,) + block, F32),
             pltpu.VMEM(block, F32),
@@ -352,15 +414,15 @@
             dma((4,)),
             dma((3,)),
             dma((4, 2, CHUNKS)),
-            dma((4, 2, CHUNKS)),
+            dma((4, 3, CHUNKS)),
             dma((2, 3, CHUNKS)),
             dma((2, 3, CHUNKS)),
             dma((3, 3)),
             dma((3, 3)),
-            dma((CHUNKS,)),
+            dma((4, CHUNKS)),
         ],
         compiler_params=pltpu.CompilerParams(
-            collective_id=0, has_side_effects=True, vmem_limit_bytes=62 << 20
+            collective_id=0, has_side_effects=True, vmem_limit_bytes=57 << 20
         ),
     )(fields, velocity, noise, mixing_rate, parcel_cell, parcel_mass, parcel_temp)
 

time: 236 us -> 187 us (0.79)
  the two profiles are of different devices: /device:TPU:3 before, /device:TPU:1 now
where the time goes in v2:
time: 187 us
  Pallas kernels  183 us (98%)
  local copies, waits for them, and re-layouts  3.72 us (2%)
    pallas_call x1, Pallas kernels, on_device(): pl.pallas_call(kernel, out_shape=(pltpu.VMEM(fields.shape, F32), pltpu.VM...  183 us

profile of v2, /device:TPU:1, one launch (start us, length us, event | category | flops | bytes accessed | tf_op | source)
XLA Modules:
  0.0 187.3 jit_solution(4189787588166341417)
XLA Ops:
  0.6 183.0 %shard_map.94 = (f32[2,22,4,32,256]{4,3,2,1,0:T(8,128)S(1)}, f32[1,1024]{1,0:T(1,128)S(1)}, f32[1,1024]{1,0:T(1,128)S(1)}) custom-call(f32[2,22,4,32,256]{4,3,2,1,0:T(8,128)} %fields_in.1, f32[3,4,32,256]{3,2,1,0:T(8,128)} %velocity_in.1, s32[2,2,2,3,4,32,256]{6,5,4,3,2,1,0:T(8,128)} %noise_in.1, f32[4,32,256]{2,1,0:T(8,128)} %mixing_in.1, ...), custom_call_target="tpu_custom_call" | custom-call | tf_op jit(solution)/shard_map/pallas_call | solution.py:388
  183.6 2.5 %copy.13 = f32[2,22,4,32,256]{4,3,2,1,0:T(8,128)} copy(f32[2,22,4,32,256]{4,3,2,1,0:T(8,128)S(1)} %get-tuple-element.3) | data formatting | bytes 11534336
  186.1 0.6 copy.14
  186.7 0.6 copy.15

commit v3 on v2

--- a/solution.py
+++ b/solution.py
@@ -21,9 +21,12 @@
 step_time = 0.4
 latent_heat = 0.5
 
-LAG_TOTAL = 3
-LAG_RELAX = 4
-LAG_PASS = 4
+FIRST_GROUP = 5
+LAG_PAIR = 1
+LAG_TOTAL = 2
+LAG_RELAX = 3
+LAG_PASS = 2
+WINDOW = 3
 
 
 def split3(value):
@@ -69,16 +72,13 @@
 
     base = s - lax.rem(s, 16)
     other = 16 - base
-    x = lax.rem(s, 16) // 4
-    upward = lax.rem(s, 4) == 3
-    downward = lax.rem(s, 4) == 0
-    edge = upward | downward
-    rank = jnp.where(upward, x, 3 - x)
-    is_relay = edge & (rank != 0)
-    is_end = edge & (rank == 3)
+    place = lax.rem(s, 16)
+    upward = place == 15
+    downward = place == 0
+    is_end = upward | downward
     relay_side = jnp.where(upward, 0, 1)
     relay_dest = {"space": base + jnp.where(upward, 0, 15)}
-    relay_source = {"space": other + jnp.where(upward, 15, 0)}
+    relay_peer = {"space": other + place}
 
     barrier = pltpu.get_barrier_semaphore()
 
@@ -88,27 +88,27 @@
     for peer in (above, below, twin, across, corner):
         greet(peer)
 
-    @pl.when(is_relay)
-    def _():
-        greet(relay_source)
-
     @pl.when(is_end)
     def _():
-        for column in range(1, 4):
-            greet({"space": base + jnp.where(upward, 4 * (3 - column), 4 * column + 3)})
-
-    pl.semaphore_wait(barrier, 5 + jnp.where(is_relay, 1, 0) + jnp.where(is_end, 3, 0))
+        greet(relay_peer)
+        greet(relay_dest)
+
+    pl.semaphore_wait(barrier, 5 + jnp.where(is_end, 2, 0))
+
+    def goes_round(phase, c):
+        if phase == 1:
+            return c >= 0
+        if phase == 3:
+            return c >= 0
+        return c < 0
 
     def halo_copy(phase, side, c):
         plane = CX - 1 if side == 0 else 0
         held = (fields_in, new, old, new)[phase]
         land, peer = side, (above if side == 0 else below)["space"]
-        if phase:
-            route = lax.rem(c, 4)
-            by_relay = is_end & (upward if side == 0 else downward) & (route != 0)
-            land = jnp.where(by_relay, 2, side)
-            column = 4 * route + 3 if side == 0 else 4 * (3 - route)
-            peer = jnp.where(by_relay, other + column, peer)
+        relayed = by_relay(phase, side, c)
+        land = jnp.where(relayed, 2, side)
+        peer = jnp.where(relayed, other + (15 if side == 0 else 0), peer)
         return pltpu.make_async_remote_copy(
             src_ref=held.at[:, pl.ds(2 * c, 2), plane],
             dst_ref=halo.at[phase, land, :, pl.ds(2 * c, 2)],
@@ -133,17 +133,28 @@
         )
 
     def relays(phase, c):
-        return is_relay & (lax.rem(c, 4) == rank)
+        return is_end & goes_round(phase, c)
 
     def pass_on(phase, c):
-        @pl.when((c >= 0) & (c < CHUNKS) & relays(phase, c))
+        @pl.when(relays(phase, c))
         def _():
             halo_arrived(phase, 2, c)
             relay_copy(phase, c).start()
 
-    def send_halo(phase, c):
+    def by_relay(phase, side, c):
+        return is_end & (upward if side == 0 else downward) & goes_round(phase, c)
+
+    def send_early(phase, c):
         for side in range(2):
-            halo_copy(phase, side, c).start()
+            @pl.when(by_relay(phase, side, c))
+            def _():
+                halo_copy(phase, side, c).start()
+
+    def send_in_turn(phase, c):
+        for side in range(2):
+            @pl.when(jnp.logical_not(by_relay(phase, side, c)))
+            def _():
+                halo_copy(phase, side, c).start()
 
     def mean_copy(step, stage, c):
         src, dst, peer = (
@@ -158,10 +169,10 @@
         )
 
     def start_halo(c, carry):
-        send_halo(0, c)
+        send_in_turn(0, c)
         return carry
 
-    lax.fori_loop(0, CHUNKS, start_halo, 0)
+    lax.fori_loop(0, FIRST_GROUP, start_halo, 0)
 
     for load in parcel_loads:
         load.wait()
@@ -177,14 +188,16 @@
     for copy in parcel_copies:
         copy.start()
 
-    def set_coef(step, sub_step):
+    def set_coef(phase):
+        step, sub_step = phase // 2, phase % 2
+
         def one(b, carry):
             for p in range(CX):
                 for d in range(3):
                     speed = velocity[d, p]
                     drift = (0.5 * noise_gain) * noise[step, sub_step, b, d, p].astype(F32)
-                    coef[b, p, 2 * d] = (sub_time * diffusivity) + sub_time * jnp.maximum(speed, 0.0) - drift
-                    coef[b, p, 2 * d + 1] = (sub_time * diffusivity) - sub_time * jnp.minimum(speed, 0.0) + drift
+                    coef[sub_step, b, p, 2 * d] = (sub_time * diffusivity) + sub_time * jnp.maximum(speed, 0.0) - drift
+                    coef[sub_step, b, p, 2 * d + 1] = (sub_time * diffusivity) - sub_time * jnp.minimum(speed, 0.0) + drift
             return carry
 
         lax.fori_loop(0, 2, one, 0)
@@ -194,7 +207,7 @@
         speeds = jnp.abs(velocity[0, p]) + jnp.abs(velocity[1, p]) + jnp.abs(velocity[2, p])
         coef_mid[p] = (1.0 - 6.0 * sub_time * diffusivity) - sub_time * speeds
     loads[1].wait()
-    set_coef(0, 0)
+    set_coef(0)
     loads[2].wait()
     loads[3].wait()
     weight[...] = step_time * weight[...]
@@ -211,12 +224,12 @@
                     upper = held[b, n, p + 1] if p < CX - 1 else halo[phase, 1, b, n]
                     made[b, n, p] = (
                         coef_mid[p] * q
-                        + coef[b, p, 0] * lower
-                        + coef[b, p, 1] * upper
-                        + coef[b, p, 2] * pltpu.roll(q, 1, 0)
-                        + coef[b, p, 3] * pltpu.roll(q, NY - 1, 0)
-                        + coef[b, p, 4] * pltpu.roll(q, 1, 1)
-                        + coef[b, p, 5] * pltpu.roll(q, NZ - 1, 1)
+                        + coef[phase % 2, b, p, 0] * lower
+                        + coef[phase % 2, b, p, 1] * upper
+                        + coef[phase % 2, b, p, 2] * pltpu.roll(q, 1, 0)
+                        + coef[phase % 2, b, p, 3] * pltpu.roll(q, NY - 1, 0)
+                        + coef[phase % 2, b, p, 4] * pltpu.roll(q, 1, 1)
+                        + coef[phase % 2, b, p, 5] * pltpu.roll(q, NZ - 1, 1)
                     )
             return carry
 
@@ -298,66 +311,94 @@
                     for b in range(2):
                         old[b, j, p] += step_time * source[j, p * NY:(p + 1) * NY]
 
-    for step in range(2):
-        if step:
-            set_coef(step, 0)
-
-        def first(c, carry):
-            if step:
-                pass_on(2, c + CHUNKS - LAG_PASS)
-            pass_on(2 * step + 1, c - LAG_PASS)
-            for side in range(2):
-                halo_arrived(2 * step, side, c)
-                if step:
-                    halo_copy(1, side, c).wait_send()
-            substep(2 * step, c)
-            send_halo(2 * step + 1, c)
-            return carry
-
-        lax.fori_loop(0, CHUNKS, first, 0)
-        set_coef(step, 1)
-
-        def second(i, carry):
-            pass_on(2 * step + 1, i + CHUNKS - LAG_PASS)
-            if step == 0:
-                pass_on(2, i - LAG_RELAX - LAG_PASS)
-
-            @pl.when(i < CHUNKS)
-            def _():
-                c = i
-                for side in range(2):
-                    halo_arrived(2 * step + 1, side, c)
-                    if step:
-                        halo_copy(2, side, c).wait_send()
-                substep(2 * step + 1, c)
-                sum_parts(step, c)
-                mean_copy(step, 0, c).start()
-
-            @pl.when((i >= 1) & (i < CHUNKS + 1))
-            def _():
-                c = i - 1
-                mean_copy(step, 0, c).wait_recv()
-                pair[step, c] = part[step, 2 * c + core] + part_land[step, c]
-                mean_copy(step, 1, c).start()
-
-            @pl.when((i >= LAG_TOTAL) & (i < CHUNKS + LAG_TOTAL))
-            def _():
-                c = i - LAG_TOTAL
-                mean_copy(step, 1, c).wait_recv()
-                mean[step, 2 * c + core] = 0.125 * (pair[step, c] + pair_land[step, c])
-                mean_copy(step, 2, c).start()
-
-            @pl.when(i >= LAG_RELAX)
-            def _():
-                c = i - LAG_RELAX
-                mean_copy(step, 2, c).wait_recv()
-                relax(step, c)
-                if step == 0:
-                    send_halo(2, c)
-
-            return carry
-
-        lax.fori_loop(0, CHUNKS + LAG_RELAX, second, 0)
+    def mean_stages(step, group, at):
+        start, count = group
+
+        @pl.when((at >= LAG_PAIR) & (at < count + LAG_PAIR))
+        def _():
+            c = start + at - LAG_PAIR
+            mean_copy(step, 0, c).wait_recv()
+            pair[step, c] = part[step, 2 * c + core] + part_land[step, c]
+            mean_copy(step, 1, c).start()
+
+        @pl.when((at >= LAG_TOTAL) & (at < count + LAG_TOTAL))
+        def _():
+            c = start + at - LAG_TOTAL
+            mean_copy(step, 1, c).wait_recv()
+            mean[step, 2 * c + core] = 0.125 * (pair[step, c] + pair_land[step, c])
+            mean_copy(step, 2, c).start()
+
+        @pl.when((at >= LAG_RELAX) & (at < count + LAG_RELAX))
+        def _():
+            c = start + at - LAG_RELAX
+            mean_copy(step, 2, c).wait_recv()
+            relax(step, c)
+
+    def guarded(group, j, act, *phase):
+        start, count = group
+
+        @pl.when((j >= 0) & (j < count))
+        def _():
+            act(*phase, start + j)
+
+    def consume(phase, c):
+        for side in range(2):
+            halo_arrived(phase, side, c)
+            if phase >= 2:
+                halo_copy(phase - 1, side, c).wait_send()
+        substep(phase, c)
+        if phase % 2:
+            sum_parts(phase // 2, c)
+            mean_copy(phase // 2, 0, c).start()
+        else:
+            send_early(phase + 1, c)
+
+    low, high = (0, FIRST_GROUP), (FIRST_GROUP, CHUNKS - FIRST_GROUP)
+    plan = (((0, low),), ((1, low), (0, high)), ((1, high), (2, low)), ((3, low), (2, high)), ((3, high),))
+    length = [max(group[1] for _, group in stage) for stage in plan]
+
+    for k, stage in enumerate(plan):
+        before = plan[k - 1] if k else ()
+        after = plan[k + 1] if k + 1 < len(plan) else ()
+        if 1 <= k <= 3:
+            set_coef(k)
+        if not after:
+            for c in range(high[0] + WINDOW, CHUNKS):
+                send_in_turn(3, c)
+
+        def body(i, carry):
+            for phase, group in before:
+                if phase % 2 == 0:
+                    guarded(group, i + length[k - 1] - LAG_PASS, pass_on, phase + 1)
+            for phase, group in stage:
+                if phase % 2 == 0:
+                    guarded(group, i - LAG_PASS, pass_on, phase + 1)
+            for phase, group in before:
+                if phase % 2:
+                    mean_stages(phase // 2, group, i + length[k - 1])
+            for phase, group in stage:
+                guarded(group, i, consume, phase)
+                if phase % 2:
+                    mean_stages(phase // 2, group, i)
+            if 0 < k < len(plan) - 1:
+                @pl.when(i < length[k] - WINDOW)
+                def _():
+                    for phase, group in stage:
+                        guarded(group, i + WINDOW, send_in_turn, phase)
+            if after:
+                @pl.when(i >= length[k] - WINDOW)
+                def _():
+                    for phase, group in after:
+                        guarded(group, i + WINDOW - length[k], send_in_turn, phase)
+            return carry
+
+        lax.fori_loop(0, length[k], body, 0)
+
+    def drain(i, carry):
+        mean_stages(1, high, i + length[-1])
+        return carry
+
+    lax.fori_loop(0, LAG_RELAX, drain, 0)
 
     mass_out[...] = masses[f]
     temp_out[...] = temps[f]
@@ -369,7 +410,7 @@
         for step in range(2):
             for stage in range(3):
                 mean_copy(step, stage, c).wait_send()
-        for phase in range(1, 4):
+        for phase in (1, 3):
             @pl.when(relays(phase, c))
             def _():
                 relay_copy(phase, c).wait_send()
@@ -400,7 +441,7 @@
             pltpu.VMEM(noise.shape, jnp.int32),
             pltpu.VMEM((3,) + block, F32),
             pltpu.VMEM(block, F32),
-            pltpu.VMEM((2, CX, 6) + plane, F32),
+            pltpu.VMEM((2, 2, CX, 6) + plane, F32),
             pltpu.VMEM(block, F32),
             pltpu.VMEM((2, S) + block, F32),
             pltpu.VMEM((2, CHUNKS) + block, F32),

time: 187 us -> 166 us (0.89)
  Pallas kernels: 183 us -> 162 us
    pallas_call x1, Pallas kernels: 183 us -> 162 us  [on_device(): pl.pallas_call(kernel, out_shape=(pltpu.VMEM(fields.shape, F32), pltpu.VM...]
where the time goes in v3:
time: 166 us
  Pallas kernels  162 us (98%)
  local copies, waits for them, and re-layouts  3.72 us (2%)
    pallas_call x1, Pallas kernels, on_device(): pl.pallas_call(kernel, out_shape=(pltpu.VMEM(fields.shape, F32), pltpu.VM...  162 us
    unnamed x3, local copies, waits for them, and re-layouts  3.72 us

profile of v3, /device:TPU:1, one launch (start us, length us, event | category | flops | bytes accessed | tf_op | source)
XLA Modules:
  0.0 165.9 jit_solution(3512999459133714213)
XLA Ops:
  0.6 161.5 %shard_map.94 = (f32[2,22,4,32,256]{4,3,2,1,0:T(8,128)S(1)}, f32[1,1024]{1,0:T(1,128)S(1)}, f32[1,1024]{1,0:T(1,128)S(1)}) custom-call(f32[2,22,4,32,256]{4,3,2,1,0:T(8,128)} %fields_in.1, f32[3,4,32,256]{3,2,1,0:T(8,128)} %velocity_in.1, s32[2,2,2,3,4,32,256]{6,5,4,3,2,1,0:T(8,128)} %noise_in.1, f32[4,32,256]{2,1,0:T(8,128)} %mixing_in.1, ...), custom_call_target="tpu_custom_call" | custom-call | tf_op jit(solution)/shard_map/pallas_call | solution.py:429
  162.2 2.5 %copy.13 = f32[2,22,4,32,256]{4,3,2,1,0:T(8,128)} copy(f32[2,22,4,32,256]{4,3,2,1,0:T(8,128)S(1)} %get-tuple-element.3) | data formatting | bytes 11534336
  164.7 0.6 copy.14
  165.3 0.6 copy.15

commit v4 on v3

--- a/solution.py
+++ b/solution.py
@@ -420,13 +420,24 @@
     lax.fori_loop(0, CHUNKS, finish, 0)
 
 
+def write_out(fields, mass, temp, fields_out, mass_out, temp_out, sem):
+    copies = [
+        pltpu.make_async_copy(held, out, sem.at[k])
+        for k, (held, out) in enumerate(((fields, fields_out), (mass, mass_out), (temp, temp_out)))
+    ]
+    for copy in copies:
+        copy.start()
+    for copy in copies:
+        copy.wait()
+
+
 def on_device(fields, velocity, noise, mixing_rate, parcel_cell, parcel_mass, parcel_temp):
     anywhere = pl.BlockSpec(memory_space=pl.ANY)
     in_vmem = pl.BlockSpec(memory_space=pltpu.VMEM)
     plane = (NY, NZ)
     block = (CX,) + plane
     dma = pltpu.SemaphoreType.DMA
-    return pl.pallas_call(
+    held = pl.pallas_call(
         kernel,
         out_shape=(
             pltpu.VMEM(fields.shape, F32),
@@ -466,6 +477,14 @@
             collective_id=0, has_side_effects=True, vmem_limit_bytes=57 << 20
         ),
     )(fields, velocity, noise, mixing_rate, parcel_cell, parcel_mass, parcel_temp)
+    return pl.pallas_call(
+        write_out,
+        out_shape=tuple(jax.ShapeDtypeStruct(array.shape, F32) for array in held),
+        in_specs=[anywhere] * 3,
+        out_specs=(anywhere,) * 3,
+        scratch_shapes=[dma((3,))],
+        compiler_params=pltpu.CompilerParams(has_side_effects=True, vmem_limit_bytes=1 << 20),
+    )(*held)
 
 
 def solution(mesh):

time: 166 us -> 165 us (level)
  local copies, waits for them, and re-layouts: 3.72 us -> 0 us
  Pallas kernels: 162 us -> 164 us
    unnamed x3 -> x0, local copies, waits for them, and re-layouts: 3.72 us -> none
    pallas_call x0 -> x1, Pallas kernels: none -> 2.56 us  [on_device(): pl.pallas_call(write_out, out_shape=tuple((jax.ShapeDtypeStruct(array.sha...]
where the time goes in v4:
time: 165 us
  Pallas kernels  164 us (99%)
    pallas_call x1, Pallas kernels, on_device(): pl.pallas_call(kernel, out_shape=(pltpu.VMEM(fields.shape, F32), pltpu.VM...  162 us

profile of v4, /device:TPU:1, one launch (start us, length us, event | category | flops | bytes accessed | tf_op | source)
XLA Modules:
  0.0 164.7 jit_solution(14185971438345510021)
XLA Ops:
  0.6 161.5 %shard_map.94 = (f32[2,22,4,32,256]{4,3,2,1,0:T(8,128)S(1)}, f32[1,1024]{1,0:T(1,128)S(1)}, f32[1,1024]{1,0:T(1,128)S(1)}) custom-call(f32[2,22,4,32,256]{4,3,2,1,0:T(8,128)} %fields_in.1, f32[3,4,32,256]{3,2,1,0:T(8,128)} %velocity_in.1, s32[2,2,2,3,4,32,256]{6,5,4,3,2,1,0:T(8,128)} %noise_in.1, f32[4,32,256]{2,1,0:T(8,128)} %mixing_in.1, ...), custom_call_target="tpu_custom_call" | custom-call | tf_op jit(solution)/shard_map/pallas_call | solution.py:440
  162.2 2.6 %shard_map.95 = (f32[2,22,4,32,256]{4,3,2,1,0:T(8,128)}, f32[1,1024]{1,0:T(1,128)}, f32[1,1024]{1,0:T(1,128)}) custom-call(f32[2,22,4,32,256]{4,3,2,1,0:T(8,128)S(1)} %get-tuple-element.6.fields, f32[1,1024]{1,0:T(1,128)S(1)} %get-tuple-element.7.mass, f32[1,1024]{1,0:T(1,128)S(1)} %get-tuple-element.8.temp), custom_call_target="tpu_custom_call" | custom-call | tf_op jit(solution)/shard_map/pallas_call | solution.py:480
